TPU v7x, 256 devices: a whole 4x4x8 slice. The times are simulated.
256 devices in a mesh: tok: 16 (over y_lo, z), voc: 16 (over y_hi, x, core).
Axes of the slice: x: 4, y: 4 (y_hi: 2, y_lo: 2; y = y_hi * 2 + y_lo), z: 8, core: 2. Of those that a mesh axis runs over, the one named last changes fastest.
Arguments:
- hidden: bfloat16 [1024, 8192], P('tok', 'voc'), may hold values from -200 to 200
- gain: float32 [8192], replicated, may hold values from 0.5 to 1.5
- head_weight: bfloat16 [8192, 131072], P(None, ('tok', 'voc')), may hold values from -10 to 10
- student: bfloat16 [1024, 131072], P(None, ('tok', 'voc')), may hold values from -30 to -2
- token_ids: int32 [1024], replicated, may hold values from 0 to 131071
- lengths: int32 [16], replicated, may hold values from 1 to 64
Outputs:
- divergence: float32 [1024], P('tok')
- token_logprob: float32 [1024], P('tok')
All inputs are finite; a program needn't handle non-finite values.
Results may differ from a plain program's by a relative error of at most 0.0023.
Values may be sent and summed in bfloat16 or wider, within the bound.
A program may use at most 128 MiB of HBM per device.

v0:
```python
import jax
import jax.numpy as jnp
from jax import lax
from jax.sharding import PartitionSpec as P

D = 8192
LEN = 64


EPS = 1e-06


def per_device(hidden, gain, head_weight, student, token_ids, lengths):
    rows_dev, width_dev = hidden.shape
    vocab_dev = head_weight.shape[1]
    voc_place = lax.axis_index("voc")
    tok_place = lax.axis_index("tok")
    hf = hidden.astype(jnp.float32)
    squares = lax.psum(jnp.sum(hf * hf, axis=1), "voc")
    gain_dev = lax.dynamic_slice_in_dim(gain, voc_place * width_dev, width_dev)
    normed = (hf * lax.rsqrt(squares / D + EPS)[:, None] * gain_dev[None, :]).astype(jnp.bfloat16)
    full_rows = lax.all_gather(normed, "voc", axis=1, tiled=True)
    logits = jnp.dot(
        lax.all_gather(full_rows, "tok", axis=0, tiled=True),
        head_weight,
        preferred_element_type=jnp.float32,
    )
    top = lax.pmax(jnp.max(logits, axis=1), ("tok", "voc"))
    total = lax.psum(jnp.sum(jnp.exp(logits - top[:, None]), axis=1), ("tok", "voc"))
    lse = top + jnp.log(total)
    shifted = logits - lse[:, None]
    kl_terms = jnp.sum(jnp.exp(shifted) * (shifted - student.astype(jnp.float32)), axis=1)
    offset = lax.axis_index(("tok", "voc")) * vocab_dev
    columns = offset + jnp.arange(vocab_dev, dtype=jnp.int32)
    picked = jnp.sum(
        jnp.where(columns[None, :] == token_ids[:, None], logits, jnp.float32(0.0)), axis=1
    )
    parts = (
        lax.psum_scatter(kl_terms, ("tok", "voc"), scatter_dimension=0, tiled=True),
        lax.psum_scatter(picked, ("tok", "voc"), scatter_dimension=0, tiled=True),
    )
    kl_block, pick_block = (
        lax.all_gather(parts[0], "voc", axis=0, tiled=True),
        lax.all_gather(parts[1], "voc", axis=0, tiled=True),
    )
    lse_block = lax.dynamic_slice_in_dim(lse, tok_place * rows_dev, rows_dev)
    positions = tok_place * rows_dev + jnp.arange(rows_dev, dtype=jnp.int32)
    sequence = positions // LEN
    seq_index = jnp.arange(lengths.shape[0], dtype=jnp.int32)
    limit = jnp.sum(jnp.where(sequence[:, None] == seq_index[None, :], lengths[None, :], 0), axis=1)
    valid = positions % LEN < limit
    divergence = jnp.where(valid, kl_block, jnp.float32(0.0))
    token_logprob = jnp.where(valid, pick_block - lse_block, jnp.float32(0.0))
    return (divergence, token_logprob)


def solution(mesh):
    placed = (P("tok", "voc"), P(), P(None, ("tok", "voc")), P(None, ("tok", "voc")), P(), P())
    return jax.shard_map(
        per_device, mesh=mesh, in_specs=placed, out_specs=(P("tok"), P("tok")), check_vma=False
    )
```

profile of v0, /device:TPU:1, one launch (start us, length us, event | category | flops | bytes accessed | tf_op | source)
XLA Modules:
  0.0 565.6 jit_solution(8149766146202457898)
XLA Ops:
  7.2 0.0 copy-start.2
  7.2 0.0 copy-start.1
  7.2 0.0 all-gather.3.cloned.1.call-start
  7.2 1.0 fusion
  8.2 35.8 %psum.14 = f32[64]{0:T(128)S(1)} all-reduce(f32[64]{0:T(128)S(1)} %fusion), channel_id=1, replica_groups=mesh['tok'=16,'voc'=16] {'voc'}, use_global_device_ids=true, to_apply=%region_2.0 | all-reduce | flops 64 | bytes 512 | tf_op jit(solution)/shard_map/psum | solution.py:19
  44.0 0.8 dynamic_slice.6
  44.7 1.5 fusion.2
  46.3 0.0 all-gather.3.cloned.1.call-update
  46.3 0.0 all-gather.5.cloned.1.call-start
  46.3 52.4 %all-gather.3.cloned.1.call-done = bf16[64,8192]{1,0:T(8,128)(2,1)} async-done(((bf16[64,512]{1,0:T(8,128)(2,1)}), bf16[64,8192]{1,0:T(8,128)(2,1)}) %all-gather.3.cloned.1.call-update) | async-done | bytes 1048592 | tf_op jit(solution)/shard_map/all_gather | solution.py:22
  98.7 0.0 all-gather.5.cloned.1.call-update
  98.8 1.5 copy.10
  100.3 0.0 copy-done.2
  100.3 0.6 dynamic-slice
  101.6 0.0 copy-done.1
  101.6 0.1 select_reduce_fusion.1
  101.7 182.6 %all-gather.5.cloned.1.call-done = bf16[1024,8192]{1,0:T(8,128)(2,1)} async-done(((bf16[64,8192]{1,0:T(8,128)(2,1)}), bf16[1024,8192]{1,0:T(8,128)(2,1)}) %all-gather.5.cloned.1.call-update) | async-done | bytes 16777232 | tf_op jit(solution)/shard_map/all_gather | solution.py:24
  284.3 17.3 %fusion.4 = (f32[1024]{0:T(1024)S(1)}, f32[1024,512]{0,1:T(8,128)S(1)}) fusion(bf16[1024,8192]{1,0:T(8,128)(2,1)} %all-gather.5.cloned.1.call-done, bf16[8192,512]{1,0:T(8,128)(2,1)} %param.8), kind=kOutput, calls=%fused_computation.24 | convolution fusion | flops 8590457856 | bytes 27267072 | tf_op jit(solution)/shard_map/dot_general | solution.py:23
  301.6 0.0 copy-start
  301.6 75.5 %pmax.7 = f32[1024]{0:T(1024)S(1)} all-reduce(f32[1024]{0:T(1024)S(1)} %get-tuple-element.10), channel_id=1, replica_groups=mesh['tok'=16,'voc'=16] {'tok','voc'}, use_global_device_ids=true, to_apply=%region_4.0 | all-reduce | flops 1024 | bytes 8192 | tf_op jit(solution)/shard_map/pmax | solution.py:28
  377.1 0.3 exponential_reduce_fusion
  377.5 73.0 %psum.15 = f32[1024]{0:T(1024)S(1)} all-reduce(f32[1024]{0:T(1024)S(1)} %exponential_reduce_fusion), channel_id=1, replica_groups=mesh['tok'=16,'voc'=16] {'tok','voc'}, use_global_device_ids=true, to_apply=%region_6.0 | all-reduce | flops 1024 | bytes 8192 | tf_op jit(solution)/shard_map/psum | solution.py:29
  450.5 0.0 copy-done
  450.5 0.7 select_reduce_fusion
  451.2 73.5 %all-reduce.4 = (f32[1024]{0:T(1024)S(1)}, f32[1024]{0:T(1024)S(1)}) all-reduce(f32[1024]{0:T(1024)S(1)} %get-tuple-element.3, f32[1024]{0:T(1024)S(1)} %get-tuple-element.2), channel_id=2, replica_groups=mesh['tok'=16,'voc'=16] {'tok','voc'}, use_global_device_ids=true, to_apply=%region_8.9.clone | all-reduce | flops 2048 | bytes 16384
  524.7 0.2 dynamic-slice_dynamic-update-slice_fusion
  524.9 0.2 dynamic-slice_dynamic-update-slice_fusion.1
  525.0 33.2 %all-reduce.5 = (f32[64]{0:T(128)S(1)}, f32[64]{0:T(128)S(1)}) all-reduce(f32[64]{0:T(128)S(1)} %dynamic-slice_dynamic-update-slice_fusion.1, f32[64]{0:T(128)S(1)} %dynamic-slice_dynamic-update-slice_fusion), channel_id=1, replica_groups=mesh['tok'=16,'voc'=16] {'voc'}, use_global_device_ids=true, to_apply=%add | all-reduce | flops 128 | bytes 1024
  558.2 0.6 subtract_select_fusion
  (6 shorter events, 0.0 us)
Async XLA Ops:
  7.2 93.1 %copy-start.2 = (u32[256]{0:T(256)S(1)}, u32[256]{0:T(256)}, u32[]{:S(2)}) copy-start(u32[256]{0:T(256)} %constant.55) | copy-start | bytes 3076
  7.2 94.4 %copy-start.1 = (s32[16]{0:T(128)S(1)}, s32[16]{0:T(128)}, u32[]{:S(2)}) copy-start(s32[16]{0:T(128)} %param.11) | copy-start | bytes 196
  7.2 91.5 %all-gather.3.cloned.1.call-start = ((), (), s32[]{:S(2)}) async-start(), calls=%async_computation | async-start | bytes 1114112 | tf_op jit(solution)/shard_map/all_gather | solution.py:22
  46.3 238.0 %all-gather.5.cloned.1.call-start = ((), (), s32[]{:S(2)}) async-start(), calls=%async_computation.1 | async-start | bytes 17825792 | tf_op jit(solution)/shard_map/all_gather | solution.py:24
  301.6 148.9 %copy-start = (s32[1024]{0:T(1024)S(1)}, s32[1024]{0:T(1024)}, u32[]{:S(2)}) copy-start(s32[1024]{0:T(1024)} %param.10) | copy-start | bytes 12292
Sparse Core Ops, SparseCore 0:
  46.4 52.2 all-gather.2
  100.5 183.6 all-gather.4
where the time goes:
time: 567 us; the launch traced here: 566 us
  blocking collectives  291 us (51%)
  waiting for transfers between devices  235 us (41%)
  matrix products  17.3 us (3%)
  between operations  14.8 us (3%)
    all_gather x1, waiting for transfers between devices, per_device(): lax.all_gather(full_rows, 'tok', axis=0, tiled=True)  183 us
    unnamed x2, blocking collectives  107 us
    pmax x1, blocking collectives, per_device(): top = lax.pmax(jnp.max(logits, axis=1), ('tok', 'voc'))  75.5 us
    psum x1, blocking collectives, per_device(): lax.psum(jnp.sum(jnp.exp(logits - top[:, None]), axis=1), ('tok', 'voc'))  73 us
    all_gather x1, waiting for transfers between devices, per_device(): full_rows = lax.all_gather(normed, 'voc', axis=1, tiled=True)  52.4 us
    psum x1, blocking collectives, per_device(): squares = lax.psum(jnp.sum(hf * hf, axis=1), 'voc')  35.8 us
    dot_general x1, matrix products, per_device(): jnp.dot(lax.all_gather(full_rows, 'tok', axis=0, tiled=True), head_weight...  17.3 us
  transfers between devices with their start and end apart: 2, of which 2 were waited for; matrix products, arithmetic and copies ran while one was open for 0% of the time, Pallas kernels for 0%

commit v1 on v0

v1 whole, which is shorter than its diff:
```python
import functools

import jax
import jax.numpy as jnp
from jax import lax
from jax.experimental import pallas as pl
from jax.experimental.pallas import tpu as pltpu
from jax.sharding import PartitionSpec as P

D = 8192
LEN = 64
EPS = 1e-06
MESH = pl.DeviceIdType.MESH
F32 = jnp.float32
BF16 = jnp.bfloat16
RING = {"y": 4, "x": 4, "z": 8}
NMSG = 40
VALL = slice(None)


def split3(value):
    hi = value.astype(BF16).astype(F32)
    rest = value - hi
    mid = rest.astype(BF16).astype(F32)
    return hi, mid, (rest - mid).astype(BF16).astype(F32)


def kernel(parts, cap, hidden, gain, lens, ids, student, head, out, *scratch):
    slabs = scratch[: len(parts)]
    (w_all, st_all, onehot, st_rows, id_cols, acc, stats, scaled, sq_buf, a2a_out, a2a_in,
     fin_out, fin_a, fin_b, local_sem, pair_sem, send_sem, recv_sem) = scratch[len(parts):]
    tok = lax.axis_index("tok")
    voc = lax.axis_index("voc")
    here = {"y": (voc // 8) * 2 + tok // 8, "x": (voc // 2) % 4, "z": tok % 8}
    core = voc % 2

    def device(place, which):
        return {"tok": (place["y"] % 2) * 8 + place["z"], "voc": ((place["y"] // 2) * 4 + place["x"]) * 2 + which}

    def moved(axis, by):
        place = dict(here)
        place[axis] = lax.rem(here[axis] + by + RING[axis], RING[axis])
        return place

    def tok_peer(step):
        return {"tok": lax.rem(tok + step, 16), "voc": voc}

    def voc_peer(step):
        return {"tok": tok, "voc": lax.rem(voc + step, 16)}

    barrier = pltpu.get_barrier_semaphore()

    def greet(step, carry):
        pl.semaphore_signal(barrier, inc=1, device_id=tok_peer(step), device_id_type=MESH)
        pl.semaphore_signal(barrier, inc=1, device_id=voc_peer(step), device_id_type=MESH)
        return carry

    lax.fori_loop(1, 16, greet, 0)
    across = {"tok": lax.rem(tok + 8, 16), "voc": lax.rem(voc + 8, 16)}
    pl.semaphore_signal(barrier, inc=1, device_id=across, device_id_type=MESH)

    def head_copy(index):
        y = (index // 16) * 2 + index % 2
        return pltpu.make_async_copy(
            head.at[index], w_all.at[(index // 2) % 2, y, (index // 4) % 4], local_sem.at[index]
        )

    student_copy = pltpu.make_async_copy(student, st_all, local_sem.at[32])
    student_copy.start()

    def load(index, carry):
        head_copy(index).start()
        return carry

    lax.fori_loop(0, 32, load, 0)

    rows = hidden[...].astype(F32)
    rows = jnp.concatenate([rows, rows], axis=0)
    turned = rows.T
    square = jnp.sum(turned * turned, axis=0, keepdims=True)
    sq_buf[0] = jnp.broadcast_to(square, (8, 128))
    gain_dev = gain[:, pl.ds(pl.multiple_of(voc * 512, 512), 512)]
    scaled[...] = (rows * gain_dev).T

    pl.semaphore_wait(barrier, 31)

    def sq_copy(step):
        return pltpu.make_async_remote_copy(
            src_ref=sq_buf.at[0], dst_ref=sq_buf.at[step], send_sem=pair_sem.at[0, step],
            recv_sem=pair_sem.at[1, step], device_id=voc_peer(step), device_id_type=MESH)

    def a2a_copy(step):
        return pltpu.make_async_remote_copy(
            src_ref=a2a_out.at[lax.rem(tok + step, 16)], dst_ref=a2a_in.at[tok], send_sem=pair_sem.at[2, step],
            recv_sem=pair_sem.at[3, step], device_id=tok_peer(step), device_id_type=MESH)

    def fin_a_copy(step):
        return pltpu.make_async_remote_copy(
            src_ref=fin_out.at[lax.rem(tok + step, 16) // 2], dst_ref=fin_a.at[step], send_sem=pair_sem.at[4, step],
            recv_sem=pair_sem.at[5, step], device_id=tok_peer(step), device_id_type=MESH)

    def fin_b_copy(step):
        return pltpu.make_async_remote_copy(
            src_ref=fin_b.at[0], dst_ref=fin_b.at[step], send_sem=pair_sem.at[6, step],
            recv_sem=pair_sem.at[7, step], device_id=voc_peer(step), device_id_type=MESH)

    def start_all(copy):
        def body(step, carry):
            copy(step).start()
            return carry
        lax.fori_loop(1, 16, body, 0)

    def recv_all(copy):
        def body(step, carry):
            copy(step).wait_recv()
            return carry
        lax.fori_loop(1, 16, body, 0)

    def sent_all(copy):
        def body(step, carry):
            copy(step).wait_send()
            return carry
        lax.fori_loop(1, 16, body, 0)

    start_all(sq_copy)

    lane = lax.broadcasted_iota(jnp.int32, (1, 128), 1)
    place_of = []
    offset = jnp.int32(0)
    for pair in range(8):
        first, second = lens[2 * pair], lens[2 * pair + 1]
        low = jnp.where(lane < first, offset + lane, -1)
        high = jnp.where(lane - 64 < second, offset + first + lane - 64, -1)
        place_of.append(jnp.where(lane < 64, low, high))
        offset = offset + first + second
    place_of = jnp.concatenate(place_of, axis=1)

    def fill(block, carry):
        start = pl.multiple_of(block * 64, 64)
        want = lax.broadcasted_iota(jnp.int32, (64, 1024), 0) + start
        onehot[pl.ds(start, 64), :] = jnp.where(want == place_of, 1.0, 0.0).astype(BF16)
        return carry

    lax.fori_loop(0, cap // 64, fill, 0)

    recv_all(sq_copy)
    total_sq = sq_buf[0]
    for step in range(1, 16):
        total_sq = total_sq + sq_buf[step]
    inv = lax.rsqrt(total_sq / D + EPS)
    normed = (scaled[...].reshape(64, 8, 128) * inv[None]).reshape(16, 32, 128).astype(BF16)
    a2a_out[...] = normed
    start_all(a2a_copy)
    a2a_in[tok] = a2a_out[tok]

    local_id = ids[...] - (tok * 16 + voc) * 512
    local_id = jnp.where((local_id >= 0) & (local_id < 512), local_id, 512)
    digits = jnp.where(lax.broadcasted_iota(jnp.int32, (16, 1024), 0) == 0, local_id // 256, local_id % 256)
    digits = digits.astype(F32).astype(BF16)
    cols = lax.dot_general(onehot[...], digits, (((1,), (1,)), ((), ())), preferred_element_type=F32)
    id_cols[...] = cols[:, 0:1] * 256.0 + cols[:, 1:2]

    recv_all(a2a_copy)
    pieces = [jnp.where(lane < 64, a2a_in[2 * pair], a2a_in[2 * pair + 1]) for pair in range(8)]
    block = jnp.concatenate(pieces, axis=1)
    packed = lax.dot_general(block, onehot[...], (((1,), (1,)), ((), ())), preferred_element_type=F32).astype(BF16)

    sends = []

    def push(number, index, src, target):
        copy = pltpu.make_async_remote_copy(
            src_ref=src, dst_ref=src, send_sem=send_sem.at[number, index], recv_sem=recv_sem.at[number, index],
            device_id=target, device_id_type=MESH)
        copy.start()
        sends.append(copy)
        return copy

    def view(number, which, y=None, x=None, z=None):
        ref = slabs[number]
        pick = [VALL if at is None else at for at in (y, x, z)]
        return ref.at[(which, *pick)]

    def plane(number, which, at, half=None):
        last = parts[number][4]
        if last == "z":
            return view(number, which, y=None if half is None else pl.ds(2 * half, 2), z=at)
        if last == "x":
            return view(number, which, y=None if half is None else pl.ds(2 * half, 2), x=at)
        return view(number, which, y=at, x=None if half is None else pl.ds(2 * half, 2))

    count = range(len(parts))
    y, x, z = here["y"], here["x"], here["z"]
    stage1 = []
    for n in count:
        lane0, wide, row0, deep, last = parts[n]
        slabs[n][core, y, x, z] = packed[row0:row0 + deep, lane0:lane0 + wide]
        first = "x" if last == "z" else "z"
        own = slabs[n].at[core, y, x, z]
        stage1.append([push(n, by, own, device(moved(first, by), core)) for by in range(1, RING[first])])

    def line(n, at, half=None):
        last = parts[n][4]
        if last == "z":
            return view(n, core, y=at, x=None if half is None else pl.ds(2 * half, 2), z=z)
        if last == "x":
            return view(n, core, y=at, x=x, z=None if half is None else pl.ds(4 * half, 4))
        return view(n, core, y=y, x=at, z=None if half is None else pl.ds(4 * half, 4))

    second = ["x" if part[4] == "y" else "y" for part in parts]
    stage2 = []
    for n in count:
        for copy in stage1[n]:
            copy.wait_recv()
        axis = second[n]
        own = line(n, here[axis])
        stage2.append([push(n, 8, own, device(moved(axis, 1), core)), push(n, 9, own, device(moved(axis, -1), core))])
    for n in count:
        axis = second[n]
        stage2[n][0].wait_recv()
        far = [push(n, 10, line(n, moved(axis, -1)[axis], 0), device(moved(axis, 1), core))]
        stage2[n][1].wait_recv()
        far.append(push(n, 11, line(n, moved(axis, 1)[axis], 1), device(moved(axis, -1), core)))
        stage2[n] = far

    mate = device(here, 1 - core)
    sibs = [[] for _ in count]
    flight = {}
    for n in count:
        for copy in stage2[n]:
            copy.wait_recv()
        axis = parts[n][4]
        for half in (0, 1):
            flight[n, 1, 0, half] = push(n, 12 + half, plane(n, core, here[axis], half), device(moved(axis, 1), core))
            flight[n, -1, 0, 1 - half] = push(
                n, 20 + half, plane(n, core, here[axis], 1 - half), device(moved(axis, -1), core))
        sibs[n].append((0, push(n, 28, plane(n, core, here[axis]), mate)))

    def multiply(n, which, by, fresh=False):
        lane0, wide, row0, deep, last = parts[n]
        at = moved(last, by)[last]
        pick = tuple(at if axis == last else VALL for axis in ("y", "x", "z"))
        deep_all = 128 // RING[last] * deep
        left = slabs[n][(which, *pick)].reshape(deep_all, wide)
        right = w_all[(which, *pick, slice(row0, row0 + deep))].reshape(deep_all, 512)
        term = lax.dot_general(left, right, (((0,), (0,)), ((), ())), preferred_element_type=F32)
        if fresh:
            acc[lane0:lane0 + wide, :] = term
        else:
            acc[lane0:lane0 + wide, :] += term

    student_copy.wait()
    st_rows[...] = jnp.dot(onehot[...], st_all[...], preferred_element_type=F32).astype(BF16)

    def loaded(index, carry):
        head_copy(index).wait()
        return carry

    lax.fori_loop(0, 32, loaded, 0)
    started = set()
    todo = []

    def due(n, which, by):
        todo.append((n, which, by))

    def work():
        while todo:
            n, which, by = todo.pop(0)
            lanes = parts[n][0]
            multiply(n, which, by, fresh=lanes not in started)
            started.add(lanes)

    for n in count:
        due(n, core, 0)
    steps = max(RING[part[4]] // 2 for part in parts)
    done_sib = [0] * len(parts)

    def drain_sibs():
        for n in count:
            while done_sib[n] < len(sibs[n]):
                by, copy = sibs[n][done_sib[n]]
                copy.wait_recv()
                due(n, 1 - core, by)
                done_sib[n] += 1

    for step in range(steps):
        late = []
        for n in count:
            axis = parts[n][4]
            last_step = RING[axis] // 2 - 1
            if step > last_step:
                continue
            order = [(1, 0), (-1, 1)] if step == last_step else [(1, 0), (-1, 1), (1, 1), (-1, 0)]
            for way, half in order:
                flight[n, way, step, half].wait_recv()
                at = moved(axis, -way * (step + 1))[axis]
                go_on = step + 1 < last_step or (step + 1 == last_step and (way, half) in ((1, 0), (-1, 1)))
                if go_on:
                    base = 12 if way == 1 else 20
                    slot = 2 * (step + 1) + (half if way == 1 else 1 - half)
                    flight[n, way, step + 1, half] = push(
                        n, base + slot, plane(n, core, at, half), device(moved(axis, way), core))
            if step == last_step:
                by = step + 1
                late.append((n, by, push(n, 29 + 2 * step, plane(n, core, moved(axis, by)[axis]), mate)))
            else:
                for way in (1, -1):
                    by = -way * (step + 1)
                    late.append((n, by, push(
                        n, 29 + 2 * step + (way == 1), plane(n, core, moved(axis, by)[axis]), mate)))
        drain_sibs()
        work()
        for n, by, copy in late:
            sibs[n].append((by, copy))
            due(n, core, by)
    work()
    drain_sibs()
    work()

    lanes128 = lax.broadcasted_iota(jnp.int32, (64, 128), 1)
    lanes512 = lax.broadcasted_iota(jnp.int32, (64, 512), 1).astype(F32)

    def partials(block, carry):
        take = pl.ds(pl.multiple_of(block * 64, 64), 64)
        logits = acc[take, :]
        top = jnp.max(logits, axis=1, keepdims=True)
        low = logits - top
        expo = jnp.exp(low)
        total = jnp.sum(expo, axis=1, keepdims=True)
        cross = jnp.sum(expo * (low - st_rows[take, :].astype(F32)), axis=1, keepdims=True)
        pick = jnp.sum(jnp.where(lanes512 == id_cols[take, :], logits, 0.0), axis=1, keepdims=True)
        table = jnp.zeros((64, 128), F32)
        for at, value in enumerate((top, total, cross, pick)):
            for digit, piece in enumerate(split3(value)):
                table = jnp.where(lanes128 == 8 * digit + at, piece, table)
        stats[take, :] = table.astype(BF16)
        return carry

    lax.fori_loop(0, cap // 64, partials, 0)
    spread = lax.dot_general(stats[...], onehot[...], (((0,), (0,)), ((), ())), preferred_element_type=F32)
    spread = spread[0:8] + spread[8:16] + spread[16:24]
    for pair in range(8):
        fin_out[pair] = spread[:, 128 * pair:128 * (pair + 1)]
    start_all(fin_a_copy)
    fin_a[0] = fin_out[tok // 2]
    recv_all(fin_a_copy)

    def combine(ref):
        every = ref[...]
        top, total, cross, pick = (every[:, k:k + 1, :] for k in range(4))
        most = jnp.max(top, axis=0, keepdims=True)
        gap = top - most
        scale = jnp.exp(gap)
        return (most[0], jnp.sum(scale * total, axis=0), jnp.sum(scale * (cross + gap * total), axis=0),
                jnp.sum(pick, axis=0))

    sub = lax.broadcasted_iota(jnp.int32, (8, 128), 0)

    def table_of(values):
        table = jnp.zeros((8, 128), F32)
        for at, value in enumerate(values):
            table = jnp.where(sub == at, value, table)
        return table

    fin_b[0] = table_of(combine(fin_a))
    start_all(fin_b_copy)
    recv_all(fin_b_copy)
    top, total, cross, pick = combine(fin_b)
    log_total = jnp.log(total)
    kl = cross / total - log_total
    logprob = pick - (top + log_total)
    inside = jnp.where(lane < 64, lane, lane - 64)
    valid = inside < lens[tok]
    result = table_of((jnp.where(valid, kl, 0.0), jnp.where(valid, logprob, 0.0)))
    out[...] = jnp.where(tok % 2 == 0, result, pltpu.roll(result, 64, 1))

    for copy in sends:
        copy.wait_send()
    for copy in (sq_copy, a2a_copy, fin_a_copy, fin_b_copy):
        sent_all(copy)


def parts_of(cap):
    if cap == 512:
        return [(0, 128, 0, 32, "x"), (128, 128, 0, 16, "x"), (256, 128, 0, 32, "y"), (128, 128, 16, 16, "y"),
                (384, 128, 0, 32, "z")]
    if cap == 640:
        return [(0, 256, 0, 32, "x"), (256, 256, 0, 32, "y"), (512, 128, 0, 32, "z")]
    return [(0, 384, 0, 32, "x"), (384, 384, 0, 32, "y"), (768, 256, 0, 32, "z")]


def run(cap, number, hidden, gain, lengths, ids, student, head):
    parts = parts_of(cap)
    vmem = pl.BlockSpec(memory_space=pltpu.VMEM)
    hbm = pl.BlockSpec(memory_space=pl.ANY)
    return pl.pallas_call(
        functools.partial(kernel, parts, cap),
        out_shape=jax.ShapeDtypeStruct((8, 128), F32),
        in_specs=[vmem, vmem, pl.BlockSpec(memory_space=pltpu.SMEM), vmem, hbm, hbm],
        out_specs=vmem,
        scratch_shapes=[pltpu.VMEM((2, 4, 4, 8, part[3], part[1]), BF16) for part in parts] + [
            pltpu.VMEM((2, 4, 4, 8, 32, 512), BF16),
            pltpu.VMEM((1024, 512), BF16),
            pltpu.VMEM((cap, 1024), BF16),
            pltpu.VMEM((cap, 512), BF16),
            pltpu.VMEM((cap, 1), F32),
            pltpu.VMEM((cap, 512), F32),
            pltpu.VMEM((cap, 128), BF16),
            pltpu.VMEM((512, 128), F32),
            pltpu.VMEM((16, 8, 128), F32),
            pltpu.VMEM((16, 32, 128), BF16),
            pltpu.VMEM((16, 32, 128), BF16),
            pltpu.VMEM((8, 8, 128), F32),
            pltpu.VMEM((16, 8, 128), F32),
            pltpu.VMEM((16, 8, 128), F32),
            pltpu.SemaphoreType.DMA((33,)),
            pltpu.SemaphoreType.DMA((8, 16)),
            pltpu.SemaphoreType.DMA((len(parts), NMSG)),
            pltpu.SemaphoreType.DMA((len(parts), NMSG)),
        ],
        compiler_params=pltpu.CompilerParams(
            collective_id=number, has_side_effects=True, vmem_limit_bytes=60 * 1024 * 1024),
        name="gathered_head_%d" % cap,
    )(hidden, gain, lengths, ids, student, head)


CAPS = (1024,)


def per_device(hidden, gain, head_weight, student, token_ids, lengths):
    args = (hidden, gain.reshape(1, D), lengths, token_ids.reshape(1, -1), student,
            head_weight.reshape(32, 8, 32, head_weight.shape[1]))
    if len(CAPS) == 1:
        table = run(CAPS[0], 0, *args)
    else:
        tokens = jnp.sum(lengths)
        which = sum((tokens > cap).astype(jnp.int32) for cap in CAPS[:-1])
        table = lax.switch(which, [functools.partial(run, cap, at) for at, cap in enumerate(CAPS)], *args)
    return table[0, :64], table[1, :64]


def solution(mesh):
    placed = (P("tok", "voc"), P(), P(None, ("tok", "voc")), P(None, ("tok", "voc")), P(), P())
    return jax.shard_map(
        per_device, mesh=mesh, in_specs=placed, out_specs=(P("tok"), P("tok")), check_vma=False
    )
```

time: 567 us -> 104 us (0.18)
  blocking collectives: 291 us -> 0 us
  waiting for transfers between devices: 235 us -> 0 us
  Pallas kernels: 0 us -> 102 us
  matrix products: 17.3 us -> 0 us
  between operations: 14.8 us -> 0.64 us
    all_gather x2 -> x0, waiting for transfers between devices: 235 us -> none  [the longest x1 183 us: per_device(): lax.all_gather(full_rows, 'tok', axis=0, tiled=True)]
    psum x2 -> x0, blocking collectives: 109 us -> none  [the longest x1 73 us: per_device(): lax.psum(jnp.sum(jnp.exp(logits - top[:, None]), axis=1), ('tok', 'voc'))]
    unnamed x2 -> x0, blocking collectives: 107 us -> none
    pallas_call x0 -> x1, Pallas kernels: none -> 102 us  [run(): pl.pallas_call(functools.partial(kernel, parts, cap), out_shape=jax.Shape...]
    pmax x1 -> x0, blocking collectives: 75.5 us -> none  [per_device(): top = lax.pmax(jnp.max(logits, axis=1), ('tok', 'voc'))]
    dot_general x1 -> x0, matrix products: 17.3 us -> none  [per_device(): jnp.dot(lax.all_gather(full_rows, 'tok', axis=0, tiled=True), head_weight...]
  transfers between devices with their start and end apart: 2 -> 0, of which waited for: 2 -> 0; matrix products, arithmetic and copies ran while one was open for 0% -> 0% of each run, Pallas kernels for 0% -> 0%
where the time goes in v1:
time: 104 us
  Pallas kernels  102 us (98%)
  local copies, waits for them, and re-layouts  1.26 us (1%)
    pallas_call x1, Pallas kernels, run(): pl.pallas_call(functools.partial(kernel, parts, cap), out_shape=jax.Shape...  102 us

profile of v1, /device:TPU:1, one launch (start us, length us, event | category | flops | bytes accessed | tf_op | source)
XLA Modules:
  0.0 104.0 jit_solution(3528268742932735217)
XLA Ops:
  0.6 102.1 %gathered_head_1024.1 = f32[8,128]{1,0:T(8,128)} custom-call(bf16[64,512]{1,0:T(8,128)(2,1)} %hidden.1, f32[1,8192]{1,0:T(1,128)} %bitcast.8, s32[16]{0:T(128)} %lens.1, s32[1,1024]{1,0:T(1,128)} %bitcast.9, bf16[1024,512]{1,0:T(8,128)(2,1)} %student.1, bf16[32,8,32,512]{3,2,1,0:T(8,128)(2,1)} %bitcast.7), custom_call_target="tpu_custom_call" | custom-call | tf_op jit(solution)/shard_map/gathered_head_1024/pallas_call | solution.py:395
  102.7 1.3 %slice_bitcast_fusion = (f32[64]{0:T(128)}, f32[64]{0:T(128)}) fusion(f32[8,128]{1,0:T(8,128)} %gathered_head_1024.1), kind=kLoop, calls=%fused_computation | loop fusion | bytes 1024 | tf_op jit(solution)/shard_map/squeeze | solution.py:438

commit v2 on v1

v2 whole, which is shorter than its diff:
```python
import functools

import jax
import jax.numpy as jnp
from jax import lax
from jax.experimental import pallas as pl
from jax.experimental.pallas import tpu as pltpu
from jax.sharding import PartitionSpec as P

D = 8192
LEN = 64
EPS = 1e-06
MESH = pl.DeviceIdType.MESH
F32 = jnp.float32
BF16 = jnp.bfloat16
RING = {"y": 4, "x": 4, "z": 8}
NMSG = 48
VALL = slice(None)


def split3(value):
    hi = value.astype(BF16).astype(F32)
    rest = value - hi
    mid = rest.astype(BF16).astype(F32)
    return hi, mid, (rest - mid).astype(BF16).astype(F32)


def blocks_of(groups):
    blocks = [[] for _ in groups]
    start = 0
    for part, count in enumerate(groups):
        for _ in range(count // 2):
            blocks[part].append((start, 128))
            start += 128
    for part, count in enumerate(groups):
        if count % 2:
            blocks[part].append((start, 64))
            start += 64
    return blocks


def kernel(groups, hidden, gain, lens, ids, student, head, out, *scratch):
    cap = 64 * sum(groups)
    blocks = blocks_of(groups)
    lasts = ("x", "y", "z")
    slabs = scratch[:3]
    (w_all, st_all, h_in, gain_in, ids_in, onehot, st_rows, id_cols, acc, stats, gcol, r_rows, sq_buf, r_buf, a2a_out,
     a2a_in, fin_out, fin_a, fin_b, local_sem, pair_sem, send_sem, recv_sem) = scratch[3:]
    tok = lax.axis_index("tok")
    voc = lax.axis_index("voc")
    here = {"y": (voc // 8) * 2 + tok // 8, "x": (voc // 2) % 4, "z": tok % 8}
    core = voc % 2
    way = 1 - 2 * core

    def device(place, which):
        return {"tok": (place["y"] % 2) * 8 + place["z"], "voc": ((place["y"] // 2) * 4 + place["x"]) * 2 + which}

    def moved(axis, by):
        place = dict(here)
        place[axis] = lax.rem(here[axis] + by + RING[axis], RING[axis])
        return place

    def tok_peer(step):
        return {"tok": lax.rem(tok + step, 16), "voc": voc}

    def voc_peer(step):
        return {"tok": tok, "voc": lax.rem(voc + step, 16)}

    def plane_peer(step):
        return device({"y": lax.rem(here["y"] + step // 4, 4), "x": lax.rem(here["x"] + step % 4, 4), "z": here["z"]}, core)

    barrier = pltpu.get_barrier_semaphore()

    def greet(step, carry):
        pl.semaphore_signal(barrier, inc=1, device_id=tok_peer(step), device_id_type=MESH)
        pl.semaphore_signal(barrier, inc=1, device_id=voc_peer(step), device_id_type=MESH)
        return carry

    lax.fori_loop(1, 16, greet, 0)
    for step in range(4, 16):
        dy, dx = step // 4, step % 4
        if dy % 2 and dx:
            pl.semaphore_signal(barrier, inc=1, device_id=plane_peer(step), device_id_type=MESH)
    across = {"tok": lax.rem(tok + 8, 16), "voc": lax.rem(voc + 8, 16)}
    pl.semaphore_signal(barrier, inc=1, device_id=across, device_id_type=MESH)

    def head_copy(index):
        y = (index // 16) * 2 + index % 2
        return pltpu.make_async_copy(
            head.at[index], w_all.at[(index // 2) % 2, y, (index // 4) % 4], local_sem.at[index]
        )

    hidden_copy = pltpu.make_async_copy(hidden, h_in, local_sem.at[32])
    gain_copy = pltpu.make_async_copy(gain, gain_in, local_sem.at[33])
    ids_copy = pltpu.make_async_copy(ids, ids_in, local_sem.at[34])
    student_copy = pltpu.make_async_copy(student, st_all, local_sem.at[35])
    hidden_copy.start()
    gain_copy.start()
    ids_copy.start()
    student_copy.start()

    def load(index, carry):
        head_copy(index).start()
        return carry

    lax.fori_loop(0, 32, load, 0)

    lane = lax.broadcasted_iota(jnp.int32, (1, 128), 1)
    place_of = []
    offset = jnp.int32(0)
    for pair in range(8):
        first, second = lens[2 * pair], lens[2 * pair + 1]
        low = jnp.where(lane < first, offset + lane, -1)
        high = jnp.where(lane - 64 < second, offset + first + lane - 64, -1)
        place_of.append(jnp.where(lane < 64, low, high))
        offset = offset + first + second
    place_of = jnp.concatenate(place_of, axis=1)

    def fill(block, carry):
        start = pl.multiple_of(block * 64, 64)
        want = lax.broadcasted_iota(jnp.int32, (64, 1024), 0) + start
        onehot[pl.ds(start, 64), :] = jnp.where(want == place_of, 1.0, 0.0).astype(BF16)
        return carry

    lax.fori_loop(0, cap // 64, fill, 0)

    hidden_copy.wait()
    rows = h_in[...].astype(F32)
    rows = jnp.concatenate([rows, rows], axis=0)
    turned = rows.T
    square = jnp.sum(turned * turned, axis=0, keepdims=True)
    sq_buf[0] = jnp.broadcast_to(square, (8, 128))
    a2a_out[...] = turned.reshape(16, 32, 128).astype(BF16)

    gain_copy.wait()

    def spread_gain(row, carry):
        wide = jnp.broadcast_to(gain_in[pl.ds(row, 1), :], (128, 128)).T
        index = row // 2
        y = (index // 16) * 2 + index % 2
        start = pl.multiple_of((row % 2) * 4, 4)
        gcol[(index // 2) % 2, y, (index // 4) % 4, pl.ds(start, 4)] = wide.reshape(4, 32, 128)
        return carry

    lax.fori_loop(0, 64, spread_gain, 0)

    def zero(block, carry):
        acc[pl.ds(pl.multiple_of(block * 64, 64), 64), :] = jnp.zeros((64, 512), F32)
        return carry

    lax.fori_loop(0, cap // 64, zero, 0)

    pl.semaphore_wait(barrier, 37)

    def sq_copy(step):
        return pltpu.make_async_remote_copy(
            src_ref=sq_buf.at[0], dst_ref=sq_buf.at[step], send_sem=pair_sem.at[0, step],
            recv_sem=pair_sem.at[1, step], device_id=voc_peer(step), device_id_type=MESH)

    def a2a_copy(step):
        return pltpu.make_async_remote_copy(
            src_ref=a2a_out.at[lax.rem(tok + step, 16)], dst_ref=a2a_in.at[tok], send_sem=pair_sem.at[2, step],
            recv_sem=pair_sem.at[3, step], device_id=tok_peer(step), device_id_type=MESH)

    def r_copy(step):
        return pltpu.make_async_remote_copy(
            src_ref=r_buf.at[tok], dst_ref=r_buf.at[tok], send_sem=pair_sem.at[8, step],
            recv_sem=pair_sem.at[9, step], device_id=tok_peer(step), device_id_type=MESH)

    def fin_a_copy(step):
        return pltpu.make_async_remote_copy(
            src_ref=fin_out.at[lax.rem(tok + step, 16) // 2], dst_ref=fin_a.at[step], send_sem=pair_sem.at[4, step],
            recv_sem=pair_sem.at[5, step], device_id=tok_peer(step), device_id_type=MESH)

    def fin_b_copy(step):
        return pltpu.make_async_remote_copy(
            src_ref=fin_b.at[0], dst_ref=fin_b.at[step], send_sem=pair_sem.at[6, step],
            recv_sem=pair_sem.at[7, step], device_id=voc_peer(step), device_id_type=MESH)

    def start_all(copy):
        def body(step, carry):
            copy(step).start()
            return carry
        lax.fori_loop(1, 16, body, 0)

    def recv_all(copy):
        def body(step, carry):
            copy(step).wait_recv()
            return carry
        lax.fori_loop(1, 16, body, 0)

    def sent_all(copy):
        def body(step, carry):
            copy(step).wait_send()
            return carry
        lax.fori_loop(1, 16, body, 0)

    start_all(a2a_copy)
    start_all(sq_copy)
    a2a_in[tok] = a2a_out[tok]

    ids_copy.wait()
    local_id = ids_in[...] - (tok * 16 + voc) * 512
    local_id = jnp.where((local_id >= 0) & (local_id < 512), local_id, 512)
    digits = jnp.where(lax.broadcasted_iota(jnp.int32, (16, 1024), 0) == 0, local_id // 256, local_id % 256)
    digits = digits.astype(F32).astype(BF16)
    cols = lax.dot_general(onehot[...], digits, (((1,), (1,)), ((), ())), preferred_element_type=F32)
    id_cols[...] = cols[:, 0:1] * 256.0 + cols[:, 1:2]
    student_copy.wait()
    st_rows[...] = jnp.dot(onehot[...], st_all[...], preferred_element_type=F32).astype(BF16)

    recv_all(a2a_copy)
    pieces = [jnp.where(lane < 64, a2a_in[2 * pair], a2a_in[2 * pair + 1]) for pair in range(8)]
    block = jnp.concatenate(pieces, axis=1)
    packed = lax.dot_general(block, onehot[...], (((1,), (1,)), ((), ())), preferred_element_type=F32)

    sends = []

    def push(number, index, src, target):
        copy = pltpu.make_async_remote_copy(
            src_ref=src, dst_ref=src, send_sem=send_sem.at[number, index], recv_sem=recv_sem.at[number, index],
            device_id=target, device_id_type=MESH)
        copy.start()
        sends.append(copy)
        return copy

    y, x, z = here["y"], here["x"], here["z"]
    own = [slab.at[core, y, x, z] for slab in slabs]
    stage1 = [[], [], []]
    for n in range(3):
        for at, (start, wide) in enumerate(blocks[n]):
            if wide == 128:
                slabs[n][core, y, x, z, 32 * at:32 * at + 32] = packed[:, start:start + 128].astype(BF16)
            else:
                base = start // 128 * 128
                both = packed[:, base:base + 128]
                flipped = pltpu.roll(both, 64, 1)
                if start == base:
                    half = jnp.where(lane < 64, both[0:16], flipped[16:32])
                else:
                    half = jnp.where(lane < 64, flipped[0:16], both[16:32])
                slabs[n][core, y, x, z, 32 * at:32 * at + 16] = half.astype(BF16)
        if n < 2:
            for by in (4, 3, 5, 2, 6, 1, 7):
                stage1[n].append(push(n, by, own[n], device(moved("z", by), core)))
        else:
            for step in (10, 2, 8, 6, 9, 11, 14, 1, 3, 4, 12, 5, 7, 13, 15):
                stage1[n].append(push(n, step, own[n], plane_peer(step)))

    mate = device(here, 1 - core)

    recv_all(sq_copy)
    total_sq = sq_buf[0]
    for step in range(1, 16):
        total_sq = total_sq + sq_buf[step]
    r_buf[tok] = lax.rsqrt(total_sq / D + EPS)
    start_all(r_copy)

    def piece(n, which, c_at, b_at):
        if n == 0:
            return slabs[0].at[which, b_at, c_at]
        return slabs[1].at[which, c_at, b_at]

    def plane(n, which, c_at):
        if n == 0:
            return slabs[0].at[which, :, c_at]
        if n == 1:
            return slabs[1].at[which, c_at]
        return slabs[2].at[which, :, :, c_at]

    def zhalf(c_at, half):
        return slabs[2].at[core, pl.ds(2 * half, 2), :, c_at]

    second = ("y", "x")
    flight = {}

    def both_ways(n, name, b_at, index):
        axis = lasts[n]
        for side in (1, -1):
            flight[n, name, side] = push(
                n, index + (side == 1), piece(n, core, here[axis], b_at), device(moved(axis, side), core))

    def go_on(n, name, b_at, index):
        axis = lasts[n]
        flight[n, name, 1].wait_recv()
        flight[n, name, -1].wait_recv()
        flight[n, name, 2] = push(
            n, index, piece(n, core, moved(axis, -way)[axis], b_at), device(moved(axis, way), core))

    def multiply(n, which, pick):
        for at, (start, wide) in enumerate(blocks[n]):
            if wide == 128:
                left = slabs[n][(which, *pick, slice(32 * at, 32 * at + 32))].reshape(-1, 128)
                depth = left.shape[0]
                factor = r_rows[0:1, start:start + 128]
                weight = gcol[(which, *pick)].reshape(depth, 128)
                left = (left.astype(F32) * factor * weight).astype(BF16)
                right = w_all[(which, *pick)].reshape(depth, 512)
                acc[start:start + 128, :] += lax.dot_general(
                    left, right, (((0,), (0,)), ((), ())), preferred_element_type=F32)
            else:
                left = slabs[n][(which, *pick, slice(32 * at, 32 * at + 16))].reshape(-1, 128)
                depth = left.shape[0]
                base = start // 128 * 128
                factor = r_rows[0:1, base:base + 128]
                flipped = pltpu.roll(factor, 64, 1)
                factor = jnp.where((lane < 64) == (start == base), factor, flipped)
                weight = jnp.where(
                    lane < 64, gcol[(which, *pick, slice(0, 16))].reshape(depth, 128),
                    gcol[(which, *pick, slice(16, 32))].reshape(depth, 128))
                left = (left.astype(F32) * factor * weight).astype(BF16)
                first = w_all[(which, *pick, slice(0, 16))].reshape(depth, 512)
                other = w_all[(which, *pick, slice(16, 32))].reshape(depth, 512)
                top = lax.dot_general(left, first, (((0,), (0,)), ((), ())), preferred_element_type=F32)
                low = lax.dot_general(left, other, (((0,), (0,)), ((), ())), preferred_element_type=F32)
                acc[start:start + 64, :] += top[0:64] + low[64:128]

    def pick_plane(n, by):
        axis = lasts[n]
        at = moved(axis, by)[axis]
        return tuple(at if axis == name else VALL for name in ("y", "x", "z"))

    def pick_piece(n, by, b_at):
        axis = lasts[n]
        at = moved(axis, by)[axis]
        return (b_at, at, VALL) if n == 0 else (at, b_at, VALL)

    todo = []

    def work(limit=99):
        while todo and limit:
            multiply(*todo.pop(0))
            limit -= 1

    waiting = []

    def to_mate(n, index, ref, pick):
        waiting.append((push(n, index, ref, mate), n, pick))

    def from_mate(limit=99):
        while waiting and limit:
            copy, n, pick = waiting.pop(0)
            copy.wait_recv()
            todo.append((n, 1 - core, pick))
            limit -= 1

    for n in (0, 1):
        for copy in stage1[n]:
            copy.wait_recv()
        axis = second[n]
        for side in (1, -1):
            flight[n, "line", side] = push(
                n, 8 + (side == 1), piece(n, core, here[lasts[n]], here[axis]), device(moved(axis, side), core))
        both_ways(n, "own", here[axis], 10)
    for copy in stage1[2]:
        copy.wait_recv()
    zwaves = {}
    for half in (0, 1):
        for side in (1, -1):
            zwaves[0, half, side] = push(
                2, 16 + half * 2 + (side == 1), zhalf(z, half), device(moved("z", side), core))
    to_mate(2, 40, plane(2, core, z), pick_plane(2, 0))

    recv_all(r_copy)
    factors = [jnp.where(lane < 64, r_buf[2 * pair], r_buf[2 * pair + 1]) for pair in range(8)]
    factors = jnp.concatenate(factors, axis=1)
    factors = jnp.concatenate([factors, factors], axis=0)
    digit_row = lax.broadcasted_iota(jnp.int32, (16, 1024), 0)
    table = jnp.zeros((16, 1024), F32)
    for digit, value in enumerate(split3(factors)):
        table = jnp.where(digit_row == digit, value, table)
    table = lax.dot_general(table.astype(BF16), onehot[...], (((1,), (1,)), ((), ())), preferred_element_type=F32)
    r_rows[...] = jnp.broadcast_to(table[0:1] + table[1:2] + table[2:3], r_rows.shape)

    def loaded(index, carry):
        head_copy(index).wait()
        return carry

    lax.fori_loop(0, 32, loaded, 0)

    def zstep(step):
        for half in (0, 1):
            for side in (1, -1):
                zwaves[step, half, side].wait_recv()
                at = moved("z", -side * (step + 1))["z"]
                if step < 2:
                    zwaves[step + 1, half, side] = push(
                        2, 16 + (step + 1) * 4 + half * 2 + (side == 1), zhalf(at, half), device(moved("z", side), core))
            if step == 2:
                zwaves[3, half, 2] = push(
                    2, 28 + half, zhalf(moved("z", -way * 3)["z"], half), device(moved("z", way), core))
        for side in (1, -1):
            by = -side * (step + 1)
            to_mate(2, 41 + step * 2 + (side == 1), plane(2, core, moved("z", by)["z"]), pick_plane(2, by))
            todo.append((2, core, pick_plane(2, by)))

    for n in (0, 1):
        axis = second[n]
        flight[n, "line", 1].wait_recv()
        flight[n, "line", -1].wait_recv()
        flight[n, "far"] = push(
            n, 12, piece(n, core, here[lasts[n]], moved(axis, -way)[axis]), device(moved(axis, way), core))
        both_ways(n, "left", moved(axis, -1)[axis], 13)
        both_ways(n, "right", moved(axis, 1)[axis], 15)
    zstep(0)
    for n in (0, 1):
        go_on(n, "own", here[second[n]], 17)
    todo.append((2, core, pick_plane(2, 0)))
    from_mate(1)
    work(2)
    for n in (0, 1):
        axis = second[n]
        flight[n, "far"].wait_recv()
        both_ways(n, "far", moved(axis, 2)[axis], 18)
        to_mate(n, 24, plane(n, core, here[lasts[n]]), pick_plane(n, 0))
        todo.append((n, core, pick_plane(n, 0)))
    zstep(1)
    work(2)
    for n in (0, 1):
        axis = second[n]
        go_on(n, "left", moved(axis, -1)[axis], 20)
        go_on(n, "right", moved(axis, 1)[axis], 21)
    zstep(2)
    from_mate(4)
    work(6)
    for n in (0, 1):
        axis = second[n]
        go_on(n, "far", moved(axis, 2)[axis], 22)
        for side in (1, -1):
            at = moved(lasts[n], side)[lasts[n]]
            to_mate(n, 25 + (side == 1), plane(n, core, at), pick_plane(n, side))
            todo.append((n, core, pick_plane(n, side)))
    from_mate(4)
    work()
    for half in (0, 1):
        zwaves[3, half, 2].wait_recv()
    to_mate(2, 47, plane(2, core, moved("z", 4)["z"]), pick_plane(2, 4))
    todo.append((2, core, pick_plane(2, 4)))
    for at, (name, by) in enumerate((("own", 0), ("left", -1), ("right", 1), ("far", 2))):
        for n in (0, 1):
            axis = second[n]
            b_at = moved(axis, by)[axis]
            flight[n, name, 2].wait_recv()
            c_at = moved(lasts[n], 2)[lasts[n]]
            to_mate(n, 27 + at, piece(n, core, c_at, b_at), pick_piece(n, 2, b_at))
            todo.append((n, core, pick_piece(n, 2, b_at)))
        from_mate(2)
        work()
    from_mate()
    work()

    lanes128 = lax.broadcasted_iota(jnp.int32, (64, 128), 1)
    lanes512 = lax.broadcasted_iota(jnp.int32, (64, 512), 1).astype(F32)

    def partials(block, carry):
        take = pl.ds(pl.multiple_of(block * 64, 64), 64)
        logits = acc[take, :]
        top = jnp.max(logits, axis=1, keepdims=True)
        low = logits - top
        expo = jnp.exp(low)
        total = jnp.sum(expo, axis=1, keepdims=True)
        cross = jnp.sum(expo * (low - st_rows[take, :].astype(F32)), axis=1, keepdims=True)
        pick = jnp.sum(jnp.where(lanes512 == id_cols[take, :], logits, 0.0), axis=1, keepdims=True)
        table = jnp.zeros((64, 128), F32)
        for at, value in enumerate((top, total, cross, pick)):
            for digit, part in enumerate(split3(value)):
                table = jnp.where(lanes128 == 8 * digit + at, part, table)
        stats[take, :] = table.astype(BF16)
        return carry

    lax.fori_loop(0, cap // 64, partials, 0)
    spread = lax.dot_general(stats[...], onehot[...], (((0,), (0,)), ((), ())), preferred_element_type=F32)
    spread = spread[0:8] + spread[8:16] + spread[16:24]
    for pair in range(8):
        fin_out[pair] = spread[:, 128 * pair:128 * (pair + 1)]
    start_all(fin_a_copy)
    fin_a[0] = fin_out[tok // 2]
    recv_all(fin_a_copy)

    def combine(ref):
        every = ref[...]
        top, total, cross, pick = (every[:, k:k + 1, :] for k in range(4))
        most = jnp.max(top, axis=0, keepdims=True)
        gap = top - most
        scale = jnp.exp(gap)
        return (most[0], jnp.sum(scale * total, axis=0), jnp.sum(scale * (cross + gap * total), axis=0),
                jnp.sum(pick, axis=0))

    sub = lax.broadcasted_iota(jnp.int32, (8, 128), 0)

    def table_of(values):
        table = jnp.zeros((8, 128), F32)
        for at, value in enumerate(values):
            table = jnp.where(sub == at, value, table)
        return table

    fin_b[0] = table_of(combine(fin_a))
    start_all(fin_b_copy)
    recv_all(fin_b_copy)
    top, total, cross, pick = combine(fin_b)
    log_total = jnp.log(total)
    kl = cross / total - log_total
    logprob = pick - (top + log_total)
    inside = jnp.where(lane < 64, lane, lane - 64)
    valid = inside < lens[tok]
    result = table_of((jnp.where(valid, kl, 0.0), jnp.where(valid, logprob, 0.0)))
    out[...] = jnp.where(tok % 2 == 0, result, pltpu.roll(result, 64, 1))

    for copy in sends:
        copy.wait_send()
    for copy in (sq_copy, a2a_copy, r_copy, fin_a_copy, fin_b_copy):
        sent_all(copy)


def run(groups, number, hidden, gain, lengths, ids, student, head):
    cap = 64 * sum(groups)
    hbm = pl.BlockSpec(memory_space=pl.ANY)
    return pl.pallas_call(
        functools.partial(kernel, groups),
        out_shape=jax.ShapeDtypeStruct((8, 128), F32),
        in_specs=[hbm, hbm, pl.BlockSpec(memory_space=pltpu.SMEM), hbm, hbm, hbm],
        out_specs=pl.BlockSpec(memory_space=pltpu.VMEM),
        scratch_shapes=[pltpu.VMEM((2, 4, 4, 8, 16 * count, 128), BF16) for count in groups] + [
            pltpu.VMEM((2, 4, 4, 8, 32, 512), BF16),
            pltpu.VMEM((1024, 512), BF16),
            pltpu.VMEM((64, 512), BF16),
            pltpu.VMEM((64, 128), F32),
            pltpu.VMEM((1, 1024), jnp.int32),
            pltpu.VMEM((cap, 1024), BF16),
            pltpu.VMEM((cap, 512), BF16),
            pltpu.VMEM((cap, 1), F32),
            pltpu.VMEM((cap, 512), F32),
            pltpu.VMEM((cap, 128), BF16),
            pltpu.VMEM((2, 4, 4, 8, 32, 128), F32),
            pltpu.VMEM((8, cap), F32),
            pltpu.VMEM((16, 8, 128), F32),
            pltpu.VMEM((16, 8, 128), F32),
            pltpu.VMEM((16, 32, 128), BF16),
            pltpu.VMEM((16, 32, 128), BF16),
            pltpu.VMEM((8, 8, 128), F32),
            pltpu.VMEM((16, 8, 128), F32),
            pltpu.VMEM((16, 8, 128), F32),
            pltpu.SemaphoreType.DMA((36,)),
            pltpu.SemaphoreType.DMA((10, 16)),
            pltpu.SemaphoreType.DMA((3, NMSG)),
            pltpu.SemaphoreType.DMA((3, NMSG)),
        ],
        compiler_params=pltpu.CompilerParams(
            collective_id=number, has_side_effects=True, vmem_limit_bytes=60 * 1024 * 1024),
        name="gathered_head_%d" % cap,
    )(hidden, gain, lengths, ids, student, head)


SPLITS = ((3, 3, 2), (6, 6, 4))


def per_device(hidden, gain, head_weight, student, token_ids, lengths):
    args = (hidden, gain.reshape(64, 128), lengths, token_ids.reshape(1, -1), student,
            head_weight.reshape(32, 8, 32, head_weight.shape[1]))
    if len(SPLITS) == 1:
        table = run(SPLITS[0], 0, *args)
    else:
        tokens = jnp.sum(lengths)
        which = sum((tokens > 64 * sum(groups)).astype(jnp.int32) for groups in SPLITS[:-1])
        table = lax.switch(which, [functools.partial(run, groups, at) for at, groups in enumerate(SPLITS)], *args)
    return table[0, :64], table[1, :64]


def solution(mesh):
    placed = (P("tok", "voc"), P(), P(None, ("tok", "voc")), P(None, ("tok", "voc")), P(), P())
    return jax.shard_map(
        per_device, mesh=mesh, in_specs=placed, out_specs=(P("tok"), P("tok")), check_vma=False
    )
```

time: 104 us -> 94.2 us (0.906)
  Pallas kernels: 102 us -> 90.5 us
  other arithmetic: 0 us -> 1.29 us
    pallas_call x1, Pallas kernels: 102 us -> 90.5 us  [run(): pl.pallas_call(functools.partial(kernel, groups), out_shape=jax.ShapeDtyp...]
    reduce_sum x0 -> x1, other arithmetic: none -> 1.29 us  [per_device(): tokens = jnp.sum(lengths)]
where the time goes in v2:
time: 94.2 us; the launch traced here: 94.1 us
  Pallas kernels  90.5 us (96%)
  other arithmetic  1.29 us (1%)
  between operations  1.29 us (1%)
    pallas_call x1, Pallas kernels, run(): pl.pallas_call(functools.partial(kernel, groups), out_shape=jax.ShapeDtyp...  90.5 us

profile of v2, /device:TPU:1, one launch (start us, length us, event | category | flops | bytes accessed | tf_op | source)
XLA Modules:
  0.0 94.1 jit_solution(7338025652940518891)
XLA Ops:
  0.6 1.3 %reduce_sum.9 = s32[]{:T(128)} reduce(s32[16]{0:T(128)} %param.13, s32[]{:T(128)} %constant.0.clone.1), dimensions={0}, to_apply=%region_0.0 | reduce | flops 15 | bytes 72 | tf_op jit(solution)/shard_map/reduce_sum | solution.py:563
  2.6 91.0 %conditional.1 = (f32[8,128]{1,0:T(8,128)S(1)}) conditional(s32[]{:T(128)} %clamp.3, (bf16[64,512]{1,0:T(8,128)(2,1)}, f32[64,128]{1,0:T(8,128)}, s32[16]{0:T(128)}, s32[1,1024]{1,0:T(1,128)}, bf16[1024,512]{1,0:T(8,128)(2,1)}, /*index=5*/bf16[32,8,32,512]{3,2,1,0:T(8,128)(2,1)}) %tuple.23, (bf16[64,512]{1,0:T(8,128)(2,1)}, f32[64,128]{1,0:T(8,128)}, ...), branch_computations={%region_1.0_spmd, %region_2.0_spmd} | conditional | bytes 8 | solution.py:565
  2.8 90.5 %gathered_head_1024.1 = f32[8,128]{1,0:T(8,128)S(1)} custom-call(bf16[64,512]{1,0:T(8,128)(2,1)} %get-tuple-element.33.hidden, f32[64,128]{1,0:T(8,128)} %get-tuple-element.34.gain, s32[16]{0:T(128)} %get-tuple-element.35.lens, s32[1,1024]{1,0:T(1,128)} %get-tuple-element.36.ids, bf16[1024,512]{1,0:T(8,128)(2,1)} %get-tuple-element.37.student, ...), custom_call_target="tpu_custom_call" | custom-call | tf_op jit(solution)/shard_map/cond/branch_1_fun/gathered_head_1024/pallas_call | solution.py:518
  93.6 0.5 slice_bitcast_fusion
